TPU v7x, 512 devices: a whole 4x8x8 slice. The times are simulated.
512 devices in a mesh: dp: 64 (over x, z, core), seq: 8 (over y).
Axes of the slice: x: 4, y: 8, z: 8, core: 2. Of those that a mesh axis runs over, the one named last changes fastest.
Arguments:
- activations: bfloat16 [64, 1024, 1216], P('dp', 'seq'), may hold values from -6 to 6
- cotangent: bfloat16 [64, 1024, 2432], P('dp', 'seq'), may hold values from -0.5 to 0.5
- timesteps: int32 [64], P('dp'), may hold values from 0 to 15
- gate_table: float32 [16, 2432], replicated, may hold values from 0.1 to 1.9
- error_in: float32 [64, 1216, 2432], P('dp', 'seq'), may hold values from -6 to 6
- seed_factor: float32 [2432, 64], P('seq'), may hold values from -6 to 6
Outputs:
- error_out: float32 [64, 1216, 2432], P('dp', 'seq')
- column_factor: float32 [2432, 64], P('seq')
All inputs are finite; a program needn't handle non-finite values.
Results may differ from a plain program's by a relative error of at most 0.00065.
Values may be sent and summed in bfloat16 or wider, within the bound.
A program may use at most 64 MiB of HBM per device.

v0:
```python
import jax
import jax.numpy as jnp
from jax import lax
from jax.sharding import PartitionSpec as P


def contract_rows(first, second):
    return lax.dot_general(
        first, second, (((0,), (0,)), ((), ())), preferred_element_type=jnp.float32
    )


def per_device(activations, cotangent, timesteps, gate_table, error_in, seed_factor):
    highest = lax.Precision.HIGHEST
    act_rows = activations[0]
    cot_rows = cotangent[0]
    memory = error_in[0]
    replicas = lax.axis_size("dp")
    step_ids = jnp.arange(gate_table.shape[0], dtype=jnp.int32)
    gate_row = jnp.sum(jnp.where(step_ids[:, None] == timesteps[0], gate_table, 0.0), 0)
    columns = lax.all_to_all(act_rows, "seq", split_axis=1, concat_axis=0, tiled=True)
    gradient = contract_rows(columns, lax.all_gather(cot_rows, "seq", axis=0, tiled=True))
    merged = gradient * gate_row + memory
    seed_whole = lax.all_gather(seed_factor, "seq", axis=0, tiled=True)
    left = jnp.dot(merged, seed_whole, precision=highest)
    left_mean = lax.psum(left, "dp") / replicas
    gram = lax.psum(jnp.dot(left_mean.T, left_mean, precision=highest), "seq")
    chol = jnp.linalg.cholesky(gram)
    ortho = lax.linalg.triangular_solve(
        chol, left_mean, left_side=False, lower=True, transpose_a=True
    )
    share_rows = seed_factor.shape[0]
    right_term = lax.dot_general(
        merged,
        ortho,
        (((0,), (0,)), ((), ())),
        precision=highest,
        preferred_element_type=jnp.float32,
    )
    factor_whole = lax.psum(right_term, ("dp", "seq")) / replicas
    factor_mine = lax.dynamic_slice_in_dim(
        factor_whole, lax.axis_index("seq") * share_rows, share_rows, 0
    )
    error_out = merged - jnp.dot(ortho, factor_whole.T, precision=highest)
    return (error_out[None], factor_mine)


def solution(mesh):
    placed = (
        P("dp", "seq", None),
        P("dp", "seq", None),
        P("dp"),
        P(),
        P("dp", "seq", None),
        P("seq", None),
    )
    return jax.shard_map(
        per_device,
        mesh=mesh,
        in_specs=placed,
        out_specs=(P("dp", "seq", None), P("seq", None)),
        check_vma=False,
    )
```

profile of v0, /device:TPU:1, one launch (start us, length us, event | category | flops | bytes accessed | tf_op | source)
XLA Modules:
  0.0 661.2 jit_solution(8799242997177361332)
XLA Ops:
  7.2 0.0 all-gather.4.cloned.1.call-start
  7.2 0.7 all-gather.4.cloned.1.call-update
  7.9 7.7 %all-to-all-start = ((bf16[128,8,152]{0,2,1:T(8,128)(2,1)}), bf16[128,8,152]{0,2,1:T(8,128)(2,1)S(1)}, u32[]{:S(2)}, u32[]{:S(2)}) async-start(bf16[128,8,152]{0,2,1:T(8,128)(2,1)} %bitcast.39), calls=%async_computation | async-start | bytes 622592 | tf_op jit(solution)/shard_map/all_to_all | solution.py:21
  15.6 0.0 all-reduce.2.cloned.1.call-start
  16.3 25.9 %all-gather.1 = f32[8,304,64]{1,2,0:T(8,128)S(1)} all-gather(f32[1,304,64]{1,2,0:T(8,128)} %bitcast.40), channel_id=1, replica_groups=mesh['dp'=64,'seq'=8] {'seq'}, dimensions={0}, use_global_device_ids=true | all-gather | bytes 700416 | tf_op jit(solution)/shard_map/all_gather | solution.py:24
  42.1 0.0 copy-start.1
  42.1 0.5 copy.15
  42.6 0.3 reshape.25
  42.9 0.2 copy-done.1
  43.0 0.1 select_reduce_fusion
  43.1 0.0 all-to-all-done
  43.2 41.4 %all-gather.4.cloned.1.call-done = bf16[1,1024,2432]{2,1,0:T(8,128)(2,1)} async-done(((bf16[1,128,2432]{2,1,0:T(8,128)(2,1)}), bf16[1,1024,2432]{2,1,0:T(8,128)(2,1)}) %all-gather.4.cloned.1.call-update) | async-done | bytes 4980752 | tf_op jit(solution)/shard_map/all_gather | solution.py:22
  84.5 3.9 fusion.5
  88.4 1.7 fusion.22
  90.1 248.7 %psum.21 = f32[152,64]{0,1:T(8,128)S(1)} all-reduce(f32[152,64]{0,1:T(8,128)S(1)} %fusion.22), channel_id=1, replica_groups=mesh['dp'=64,'seq'=8] {'dp'}, use_global_device_ids=true, to_apply=%region_1.2 | all-reduce | flops 9728 | bytes 77824 | tf_op jit(solution)/shard_map/psum | solution.py:26
  338.7 0.2 fusion.13
  339.0 21.0 %psum.22 = f32[64,64]{0,1:T(8,128)S(1)} all-reduce(f32[64,64]{0,1:T(8,128)S(1)} %fusion.13), channel_id=1, replica_groups=mesh['dp'=64,'seq'=8] {'seq'}, use_global_device_ids=true, to_apply=%region_2.3 | all-reduce | flops 4096 | bytes 32768 | tf_op jit(solution)/shard_map/psum | solution.py:27
  359.9 0.1 copy.17
  360.0 5.8 cholesky.16
  365.9 0.6 compare_reduce_fusion
  366.5 0.7 fusion.15
  367.2 4.9 custom-call.6
  372.1 0.3 fusion.11
  372.4 1.8 fusion.23
  374.2 0.0 all-reduce.2.cloned.1.call-update
  374.2 275.6 %all-reduce.2.cloned.1.call-done = f32[2432,64]{0,1:T(8,128)} async-done(((f32[2432,64]{0,1:T(8,128)}), f32[2432,64]{0,1:T(8,128)}) %all-reduce.2.cloned.1.call-update) | async-done | bytes 622608 | tf_op jit(solution)/shard_map/psum | solution.py:40
  649.9 0.0 copy-start
  649.9 1.2 broadcast_multiply_fusion
  651.1 0.7 constant_dynamic-slice_fusion
  651.8 0.0 copy-done
  651.8 2.5 fusion.8
  (3 shorter events, 0.0 us)
Async XLA Ops:
  7.2 77.4 %all-gather.4.cloned.1.call-start = ((), (), s32[]{:S(2)}) async-start(), calls=%async_computation.2 | async-start | bytes 5603328 | tf_op jit(solution)/shard_map/all_gather | solution.py:22
  7.9 35.2 %all-to-all-start = ((bf16[128,8,152]{0,2,1:T(8,128)(2,1)}), bf16[128,8,152]{0,2,1:T(8,128)(2,1)S(1)}, u32[]{:S(2)}, u32[]{:S(2)}) async-start(bf16[128,8,152]{0,2,1:T(8,128)(2,1)} %bitcast.39), calls=%async_computation | async-start | bytes 622592 | tf_op jit(solution)/shard_map/all_to_all | solution.py:21
  15.6 634.3 %all-reduce.2.cloned.1.call-start = ((), (), s32[]{:S(2)}) async-start(), calls=%async_computation.1 | async-start | bytes 1245184 | tf_op jit(solution)/shard_map/psum | solution.py:40
  42.1 0.9 copy-start.1
  649.9 1.9 copy-start
Sparse Core Ops, SparseCore 0:
  10.1 74.4 all-gather.3
  374.3 275.4 all-reduce.1
where the time goes:
time: 662 us; the launch traced here: 661 us
  waiting for transfers between devices  318 us (48%)
  blocking collectives  296 us (45%)
  between operations  14.8 us (2%)
  other arithmetic  13.4 us (2%)
  matrix products  10.3 us (2%)
  starting transfers between devices  7.74 us (1%)
    psum x1, waiting for transfers between devices, per_device(): factor_whole = lax.psum(right_term, ('dp', 'seq')) / replicas  276 us
    psum x1, blocking collectives, per_device(): left_mean = lax.psum(left, 'dp') / replicas  249 us
    all_gather x1, waiting for transfers between devices, per_device(): lax.all_gather(cot_rows, 'seq', axis=0, tiled=True)  41.4 us
    all_gather x1, blocking collectives, per_device(): seed_whole = lax.all_gather(seed_factor, 'seq', axis=0, tiled=True)  25.9 us
    psum x1, blocking collectives, per_device(): gram = lax.psum(jnp.dot(left_mean.T, left_mean, precision=highest), 'seq')  21 us
  transfers between devices with their start and end apart: 3, of which 2 were waited for; matrix products, arithmetic and copies ran while one was open for 0% of the time, Pallas kernels for 0%

commit v1 on v0

v1 whole, which is shorter than its diff:
```python
import functools

import jax
import jax.numpy as jnp
from jax import lax
from jax.experimental import pallas as pl
from jax.experimental.pallas import tpu as pltpu
from jax.sharding import PartitionSpec as P

MESH = pl.DeviceIdType.MESH
F32 = jnp.float32
BF16 = jnp.bfloat16
NX, NZ, NC, NY = 4, 8, 2, 8
RANK = 64
DIN, DOUT = 1216, 2432
ROWS = DIN // NY
COLS = DOUT // NY
HALF = DIN // 2
SEED_PART = 160
SEED_SKIP = COLS - SEED_PART

LEFT_PLAN = (320, 80, 16)
RIGHT_PLAN = (608, 152, 24)


def split(value):
    high = value.astype(BF16)
    return high, (value - high.astype(F32)).astype(BF16)


def mm(first, second, dims=((1,), (0,))):
    return lax.dot_general(first, second, (dims, ((), ())), preferred_element_type=F32)


def place():
    replica = lax.axis_index("dp")
    return replica // (NZ * NC), (replica // NC) % NZ, replica % NC, lax.axis_index("seq")


def peers(axis):
    x, z, c, y = place()
    count = {"x": NX, "z": NZ, "core": NC, "y": NY}[axis]
    for step in range(1, count):
        if axis == "x":
            other = lax.rem(x + step, NX)
            yield other, (other * (NZ * NC) + z * NC + c, y)
        elif axis == "z":
            other = lax.rem(z + step, NZ)
            yield other, (x * (NZ * NC) + other * NC + c, y)
        elif axis == "core":
            other = 1 - c
            yield other, (x * (NZ * NC) + z * NC + other, y)
        else:
            other = lax.rem(y + step, NY)
            yield other, (x * (NZ * NC) + z * NC + c, other)


def exchange(axis, make, send_sems, recv_sems, during=None):
    copies = []
    for index, (other, device) in enumerate(peers(axis)):
        source, target = make(other)
        copy = pltpu.make_async_remote_copy(
            src_ref=source,
            dst_ref=target,
            send_sem=send_sems.at[index],
            recv_sem=recv_sems.at[index],
            device_id=device,
            device_id_type=MESH,
        )
        copy.start()
        copies.append(copy)
    if during is not None:
        during()
    for copy in copies:
        copy.wait()


def sum_everywhere(plan, local, bufs, sems, during):
    half_rows, x_rows, z_rows = plan
    from_core, half_sum, from_x, x_sum, from_z, z_sum, from_y, gather_z, total = bufs
    x, z, c, y = place()

    def sem(stage):
        return sems.at[0, stage], sems.at[1, stage]

    def part(index, rows):
        return pl.ds(pl.multiple_of(index * rows, 8), rows)

    exchange("core", lambda o: (local.at[part(o, half_rows)], from_core), *sem(0), during[0])
    half_sum[...] = local[part(c, half_rows), :] + from_core[...]

    exchange("x", lambda o: (half_sum.at[part(o, x_rows)], from_x.at[x]), *sem(1), during[1])
    from_x[x] = half_sum[part(x, x_rows), :]
    x_sum[0:x_rows, :] = (from_x[0] + from_x[1]) + (from_x[2] + from_x[3])

    exchange("z", lambda o: (x_sum.at[part(o, z_rows)], from_z.at[z]), *sem(2), during[2])
    from_z[z] = x_sum[part(z, z_rows), :]
    z_sum[...] = jnp.sum(from_z[...], axis=0)

    exchange("y", lambda o: (z_sum, from_y.at[y]), *sem(3), during[3])
    from_y[y] = z_sum[...]
    gather_z[z] = jnp.sum(from_y[...], axis=0)

    exchange("z", lambda o: (gather_z.at[z], gather_z.at[z]), *sem(4), during[4])
    total[part(c * NX + x, x_rows), :] = gather_z[...].reshape(NZ * z_rows, 128)[0:x_rows]

    mine = total.at[part(c * NX + x, x_rows)]
    exchange("x", lambda o: (mine, mine), *sem(5), during[5])

    mine_half = total.at[part(c, half_rows)]
    exchange("core", lambda o: (mine_half, mine_half), *sem(6), during[6])


def kernel(
    step_ref, table_ref, cot_ref, act_ref, mem_ref, seed_ref,
    ortho_ref, factor_ref,
    gate_ref, seed_mine, seed_other, seed_all, lhs, act4, left_rows, work, inverse,
    local1, core1, half1, x1, xs1, z1, zs1, y1, g1, total1,
    local2, core2, half2, x2, xs2, z2, zs2, y2, g2, total2,
    seed_sems, sems1, sems2,
):
    x, z, c, y = place()
    barrier = pltpu.get_barrier_semaphore()
    count = 0
    for axis in ("core", "x", "z", "y"):
        for _, device in peers(axis):
            pl.semaphore_signal(barrier, inc=1, device_id=device, device_id_type=MESH)
            count += 1
    pl.semaphore_wait(barrier, count)

    high, low = split(seed_ref[...])
    both = jnp.concatenate([high.astype(F32), low.astype(F32)], axis=0)
    packed = both.T.astype(BF16)
    seed_mine[y] = jnp.where(c == 0, packed[0:SEED_PART], packed[SEED_SKIP:COLS])

    def prepare():
        row = lax.broadcasted_iota(jnp.int32, table_ref.shape, 0)
        gate_ref[...] = jnp.sum(
            jnp.where(row == step_ref[0], table_ref[...], 0.0), axis=0, keepdims=True
        )
        gated_high, gated_low = split(cot_ref[...].astype(F32) * gate_ref[...])
        lhs[0:128, :] = gated_high
        lhs[128:256, :] = gated_low
        mem_high, mem_low = split(mem_ref[...])
        lhs[256 : 256 + ROWS, :] = mem_high
        lhs[416 : 416 + ROWS, :] = mem_low
        top, bottom = act_ref[0:HALF, :], act_ref[HALF:DIN, :]
        act4[:, 0:128] = top
        act4[:, 128:256] = top
        act4[:, 256:384] = bottom
        act4[:, 384:512] = bottom
        xs1[...] = jnp.zeros_like(xs1)
        xs2[...] = jnp.zeros_like(xs2)

    exchange(
        "y", lambda o: (seed_mine.at[y], seed_mine.at[y]),
        seed_sems.at[0, 0], seed_sems.at[1, 0], prepare,
    )
    exchange(
        "core", lambda o: (seed_mine, seed_other), seed_sems.at[0, 1], seed_sems.at[1, 1]
    )
    for block in range(NY):
        mine, other = seed_mine[block], seed_other[block]
        start = block * COLS
        seed_all[start : start + SEED_PART, :] = jnp.where(c == 0, mine, other)
        seed_all[start + SEED_PART : start + COLS, :] = jnp.where(
            c == 0, other, mine
        )[SEED_PART - SEED_SKIP : SEED_PART]

    product = mm(lhs[...], seed_all[...])
    tokens = product[0:128] + product[128:256]
    tokens = tokens[:, 0:RANK] + tokens[:, RANK:128]
    memory = product[256 : 256 + ROWS] + product[416 : 416 + ROWS]
    memory = memory[:, 0:RANK] + memory[:, RANK:128]
    tok_high, tok_low = split(tokens)
    column = jnp.concatenate([tok_high, tok_low], axis=0)
    blank = jnp.zeros_like(column)
    weights = jnp.concatenate(
        [
            jnp.concatenate([column, blank], axis=1),
            jnp.concatenate([blank, column], axis=1),
        ],
        axis=0,
    )
    local1[0:HALF, :] = mm(act4[...], weights)
    local1[HALF:640, :] = jnp.zeros((640 - HALF, 128), F32)
    my_rows = pl.ds(pl.multiple_of(lax.rem(y, 4) * ROWS, 8), ROWS)
    lane_half = lax.broadcasted_iota(jnp.int32, (ROWS, 128), 1) // RANK
    twice = jnp.concatenate([memory, memory], axis=1)
    local1[my_rows, :] = local1[my_rows, :] + jnp.where(lane_half == y // 4, twice, 0.0)

    sum_everywhere(
        LEFT_PLAN, local1, (core1, half1, x1, xs1, z1, zs1, y1, g1, total1), sems1, [None] * 7
    )

    left_high, left_low = split(total1[0:HALF, :])
    left_rows[0:HALF, :] = jnp.concatenate(
        [left_high[:, 0:RANK], left_low[:, 0:RANK]], axis=1
    )
    left_rows[HALF:DIN, :] = jnp.concatenate(
        [left_high[:, RANK:128], left_low[:, RANK:128]], axis=1
    )
    through = mm(left_rows[...], act_ref[...], ((0,), (0,)))
    through = through[0:RANK] + through[RANK:128]
    thr_high, thr_low = split(through)
    thr_both = jnp.concatenate([thr_high, thr_low], axis=0)
    pair = total1[my_rows, :]
    left_mine = jnp.where(y // 4 == 0, pair[:, 0:RANK], pair[:, RANK:128])
    mine_high, mine_low = split(left_mine)
    mine_both = jnp.concatenate([mine_high, mine_low], axis=1)
    for first, last in ((0, 4), (4, 8), (8, 12), (12, 16), (16, 19)):
        cols = slice(first * 128, last * 128)
        by_token = mm(thr_both, cot_ref[:, cols])
        by_high = mm(mine_both, lhs[256 : 256 + ROWS, cols], ((0,), (0,)))
        by_low = mm(mine_high, lhs[416 : 416 + ROWS, cols], ((0,), (0,)))
        right = (by_token[0:RANK] + by_token[RANK:128]) * gate_ref[:, cols]
        right = right + (by_high[0:RANK] + by_high[RANK:128]) + by_low
        for tile in range(first, last):
            at = (tile - first) * 128
            local2[tile * RANK : (tile + 1) * RANK, :] = right[:, at : at + 128]

    def gram():
        grams = mm(left_rows[...], left_rows[...], ((0,), (0,)))
        grams = grams[0:RANK] + grams[RANK:128]
        grams = grams[:, 0:RANK] + grams[:, RANK:128]
        row = lax.broadcasted_iota(jnp.int32, (RANK, RANK), 0)
        col = lax.broadcasted_iota(jnp.int32, (RANK, RANK), 1)
        work[...] = jnp.concatenate([grams, jnp.where(row == col, 1.0, 0.0)], axis=1)

    def eliminate(first, last):
        def step(k, carry):
            row = lax.broadcasted_iota(jnp.int32, (RANK, 128), 0)
            lane = lax.broadcasted_iota(jnp.int32, (RANK, 128), 1)
            whole = work[...]
            pivot_row = work[pl.ds(k, 1), :]
            column = jnp.sum(jnp.where(lane == k, whole, 0.0), axis=1, keepdims=True)
            pivot = jnp.sum(
                jnp.where(lane[0:1] == k, pivot_row, 0.0), axis=1, keepdims=True
            )
            ratio = jnp.where(row[:, 0:1] > k, column / pivot, 0.0)
            work[...] = whole - ratio * pivot_row
            return carry

        lax.fori_loop(first, last, step, 0)

    def finish():
        whole = work[...]
        row = lax.broadcasted_iota(jnp.int32, (RANK, 128), 0)
        lane = lax.broadcasted_iota(jnp.int32, (RANK, 128), 1)
        pivots = jnp.sum(jnp.where(row == lane, whole, 0.0), axis=1, keepdims=True)
        inverse[...] = whole[:, RANK:128] / jnp.sqrt(pivots)

    sum_everywhere(
        RIGHT_PLAN, local2, (core2, half2, x2, xs2, z2, zs2, y2, g2, total2), sems2,
        [
            gram,
            lambda: eliminate(0, 16),
            lambda: eliminate(16, 32),
            lambda: eliminate(32, 48),
            lambda: eliminate(48, 64),
            finish,
            None,
        ],
    )

    inv = inverse[...]
    inv_high, inv_low = split(inv)
    inv_lhs = jnp.concatenate(
        [inv_high.astype(F32), inv_high.astype(F32), inv_low.astype(F32)], axis=1
    ).astype(BF16)
    for tile in range(DOUT // 128):
        high, low = split(total2[tile * RANK : (tile + 1) * RANK, :])
        rhs = jnp.concatenate([high, low, high], axis=0)
        factor_ref[:, tile * 128 : (tile + 1) * 128] = mm(inv_lhs, rhs) * (1.0 / 64)
    ortho_ref[...] = lax.dot_general(
        left_mine, inv, (((1,), (1,)), ((), ())),
        precision=lax.Precision.HIGHEST, preferred_element_type=F32,
    )


def plan_scratch(plan):
    half_rows, x_rows, z_rows = plan
    return [
        pltpu.VMEM((2 * half_rows, 128), F32),
        pltpu.VMEM((half_rows, 128), F32),
        pltpu.VMEM((half_rows, 128), F32),
        pltpu.VMEM((NX, x_rows, 128), F32),
        pltpu.VMEM((NZ * z_rows, 128), F32),
        pltpu.VMEM((NZ, z_rows, 128), F32),
        pltpu.VMEM((z_rows, 128), F32),
        pltpu.VMEM((NY, z_rows, 128), F32),
        pltpu.VMEM((NZ, z_rows, 128), F32),
        pltpu.VMEM((2 * half_rows, 128), F32),
    ]


def factors(timesteps, gate_table, cot, act_t, memory, seed_t):
    vmem = pl.BlockSpec(memory_space=pltpu.VMEM)
    return pl.pallas_call(
        kernel,
        out_shape=(
            jax.ShapeDtypeStruct((ROWS, RANK), F32),
            jax.ShapeDtypeStruct((RANK, DOUT), F32),
        ),
        in_specs=[pl.BlockSpec(memory_space=pltpu.SMEM)] + [vmem] * 5,
        out_specs=(vmem, vmem),
        scratch_shapes=[
            pltpu.VMEM((1, DOUT), F32),
            pltpu.VMEM((NY, SEED_PART, 128), BF16),
            pltpu.VMEM((NY, SEED_PART, 128), BF16),
            pltpu.VMEM((DOUT, 128), BF16),
            pltpu.VMEM((576, DOUT), BF16),
            pltpu.VMEM((HALF, 512), BF16),
            pltpu.VMEM((DIN, 128), BF16),
            pltpu.VMEM((RANK, 128), F32),
            pltpu.VMEM((RANK, RANK), F32),
        ]
        + plan_scratch(LEFT_PLAN)
        + plan_scratch(RIGHT_PLAN)
        + [
            pltpu.SemaphoreType.DMA((2, 2, 7)),
            pltpu.SemaphoreType.DMA((2, 7, 7)),
            pltpu.SemaphoreType.DMA((2, 7, 7)),
        ],
        compiler_params=pltpu.CompilerParams(
            collective_id=0, has_side_effects=True, vmem_limit_bytes=48 * 2**20
        ),
    )(timesteps, gate_table, cot, act_t, memory, seed_t)


def per_device(activations, cotangent, timesteps, gate_table, error_in, seed_factor):
    act_rows = activations[0]
    cot_rows = cotangent[0]
    memory = error_in[0]
    step_ids = jnp.arange(gate_table.shape[0], dtype=jnp.int32)
    gate_row = jnp.sum(jnp.where(step_ids[:, None] == timesteps[0], gate_table, 0.0), 0)
    columns = lax.all_to_all(act_rows, "seq", split_axis=1, concat_axis=0, tiled=True)
    cot_all = lax.all_gather(cot_rows, "seq", axis=0, tiled=True)
    ortho, factor_t = factors(
        timesteps, gate_table, cot_rows, act_rows.T, memory, seed_factor.T
    )
    gradient = mm(columns, cot_all, ((0,), (0,)))
    merged = gradient * gate_row + memory
    error_out = merged - jnp.dot(ortho, factor_t, precision=lax.Precision.HIGHEST)
    factor_mine = lax.dynamic_slice_in_dim(
        factor_t, lax.axis_index("seq") * COLS, COLS, 1
    ).T
    return error_out[None], factor_mine


def solution(mesh):
    placed = (
        P("dp", "seq", None),
        P("dp", "seq", None),
        P("dp"),
        P(),
        P("dp", "seq", None),
        P("seq", None),
    )
    return jax.shard_map(
        per_device,
        mesh=mesh,
        in_specs=placed,
        out_specs=(P("dp", "seq", None), P("seq", None)),
        check_vma=False,
    )
```

time: 662 us -> 127 us (0.19)
  waiting for transfers between devices: 318 us -> 0.7 us
  blocking collectives: 296 us -> 0 us
  Pallas kernels: 0 us -> 93.2 us
  other arithmetic: 13.4 us -> 0.11 us
    psum x1 -> x0, waiting for transfers between devices: 276 us -> none  [per_device(): factor_whole = lax.psum(right_term, ('dp', 'seq')) / replicas]
    psum x2 -> x0, blocking collectives: 270 us -> none  [the longest x1 249 us: per_device(): left_mean = lax.psum(left, 'dp') / replicas]
    pallas_call x0 -> x1, Pallas kernels: none -> 93.2 us  [factors(): pl.pallas_call(kernel, out_shape=(jax.ShapeDtypeStruct((ROWS, RANK), F32)...]
    all_gather x1, waiting for transfers between devices: 41.4 us -> 0.02 us  [per_device(): cot_all = lax.all_gather(cot_rows, 'seq', axis=0, tiled=True)]
    all_gather x1 -> x0, blocking collectives: 25.9 us -> none  [per_device(): seed_whole = lax.all_gather(seed_factor, 'seq', axis=0, tiled=True)]
    another operation x5 -> x0, other arithmetic: 12.1 us -> none  [the longest x3 6.52 us: per_device(): chol = jnp.linalg.cholesky(gram)]
  transfers between devices with their start and end apart: 3 -> 2, of which waited for: 2 -> 0; matrix products, arithmetic and copies ran while one was open for 0% -> 1% of each run, Pallas kernels for 0% -> 74%
where the time goes in v1:
time: 127 us; the launch traced here: 126 us
  Pallas kernels  93.2 us (73%)
  between operations  14.8 us (12%)
  starting transfers between devices  7.7 us (6%)
  matrix products  5.96 us (5%)
  local copies, waits for them, and re-layouts  3.93 us (3%)
    pallas_call x1, Pallas kernels, factors(): pl.pallas_call(kernel, out_shape=(jax.ShapeDtypeStruct((ROWS, RANK), F32)...  93.2 us
    all_to_all x1, starting transfers between devices, per_device(): lax.all_to_all(act_rows, 'seq', split_axis=1, concat_axis=0, tiled=True)  7.66 us
    dot_general x1, matrix products, mm(): lax.dot_general(first, second, (dims, ((), ())), preferred_element_type=F32)  3.44 us
    unnamed x12, local copies, waits for them, and re-layouts  3.19 us
  transfers between devices with their start and end apart: 2, of which 0 were waited for; matrix products, arithmetic and copies ran while one was open for 1% of the time, Pallas kernels for 74%

profile of v1, /device:TPU:1, one launch (start us, length us, event | category | flops | bytes accessed | tf_op | source)
XLA Modules:
  0.0 126.3 jit_solution(15009118654141160419)
XLA Ops:
  7.2 0.0 copy-start.2
  7.2 0.0 copy-start.3
  7.2 0.0 all-gather.3.cloned.1.call-start
  7.2 0.7 all-gather.3.cloned.1.call-update
  7.9 7.7 %all-to-all-start = ((bf16[128,8,152]{0,2,1:T(8,128)(2,1)}), bf16[128,8,152]{0,2,1:T(8,128)(2,1)S(1)}, u32[]{:S(2)}, u32[]{:S(2)}) async-start(bf16[128,8,152]{0,2,1:T(8,128)(2,1)} %bitcast.33), calls=%async_computation | async-start | bytes 622592 | tf_op jit(solution)/shard_map/all_to_all | solution.py:337
  16.2 0.0 copy-done.2
  16.2 0.0 copy-done.3
  16.3 0.0 copy-start
  16.3 1.4 %copy-done = f32[1,152,2432]{2,1,0:T(8,128)S(1)} copy-done((f32[1,152,2432]{2,1,0:T(8,128)S(1)}, f32[1,152,2432]{2,1,0:T(8,128)}, u32[]{:S(2)}) %copy-start) | copy-done | bytes 1478680
  17.6 0.0 copy-start.4
  17.6 0.9 copy-done.4
  18.5 0.0 copy-start.5
  18.5 0.9 copy-done.5
  19.4 0.0 copy-start.1
  19.4 93.2 %shard_map.77 = (f32[152,64]{1,0:T(8,128)S(1)}, f32[64,2432]{1,0:T(8,128)S(1)}) custom-call(s32[1]{0:T(128)} %copy.15.step_ref, f32[16,2432]{1,0:T(8,128)S(1)} %copy-done.4, bf16[128,2432]{1,0:T(8,128)(2,1)S(1)} %bitcast.32, bf16[1216,128]{1,0:T(8,128)(2,1)S(1)} %bitcast.34, f32[152,2432]{1,0:T(8,128)S(1)} %bitcast.31, f32[64,304]{1,0:T(8,128)S(1)} %bitcast.35), custom_call_target="tpu_custom_call" | custom-call | tf_op jit(solution)/shard_map/pallas_call | solution.py:299
  112.6 0.7 dynamic-slice_bitcast_fusion
  113.4 0.1 select_reduce_fusion
  113.5 0.0 all-to-all-done
  113.5 0.0 all-gather.3.cloned.1.call-done
  113.5 0.0 copy-done.1
  113.5 3.4 %fusion.5 = f32[152,2432]{1,0:T(8,128)S(1)} fusion(bf16[1,1024,2432]{2,1,0:T(8,128)(2,1)} %all-gather.3.cloned.1.call-done, f32[2432]{0:T(1024)S(1)} %select_reduce_fusion, f32[1,152,2432]{2,1,0:T(8,128)S(1)} %copy-done.1, bf16[128,8,152]{0,2,1:T(8,128)(2,1)S(1)} %all-to-all-done), kind=kOutput, calls=%fused_computation.4 | convolution fusion | flops 757811200 | bytes 8259072 | tf_op jit(solution)/shard_map/dot_general | solution.py:32
  117.0 2.5 %fusion.8 = f32[1,152,2432]{2,1,0:T(8,128)} fusion(f32[152,2432]{1,0:T(8,128)S(1)} %fusion.5, f32[152,64]{1,0:T(8,128)S(1)} %get-tuple-element.4, f32[64,2432]{1,0:T(8,128)S(1)} %get-tuple-element.5), kind=kOutput, calls=%fused_computation.5 | convolution fusion | flops 284271616 | bytes 3618816 | tf_op jit(solution)/shard_map/dot_general | solution.py:344
  (1 shorter events, 0.0 us)
Async XLA Ops:
  7.2 9.1 %copy-start.2 = (bf16[1,128,2432]{2,1,0:T(8,128)(2,1)S(1)}, bf16[1,128,2432]{2,1,0:T(8,128)(2,1)}, u32[]{:S(2)}) copy-start(bf16[1,128,2432]{2,1,0:T(8,128)(2,1)} %param.7) | copy-start | bytes 1867780
  7.2 9.1 %copy-start.3 = (bf16[1,128,1216]{1,2,0:T(8,128)(2,1)S(1)}, bf16[1,128,1216]{1,2,0:T(8,128)(2,1)}, u32[]{:S(2)}) copy-start(bf16[1,128,1216]{1,2,0:T(8,128)(2,1)} %param.6) | copy-start | bytes 933892
  7.2 106.3 %all-gather.3.cloned.1.call-start = ((), (), s32[]{:S(2)}) async-start(), calls=%async_computation.1 | async-start | bytes 5603328 | tf_op jit(solution)/shard_map/all_gather | solution.py:338
  7.9 105.6 %all-to-all-start = ((bf16[128,8,152]{0,2,1:T(8,128)(2,1)}), bf16[128,8,152]{0,2,1:T(8,128)(2,1)S(1)}, u32[]{:S(2)}, u32[]{:S(2)}) async-start(bf16[128,8,152]{0,2,1:T(8,128)(2,1)} %bitcast.33), calls=%async_computation | async-start | bytes 622592 | tf_op jit(solution)/shard_map/all_to_all | solution.py:337
  16.3 1.4 %copy-start = (f32[1,152,2432]{2,1,0:T(8,128)S(1)}, f32[1,152,2432]{2,1,0:T(8,128)}, u32[]{:S(2)}) copy-start(f32[1,152,2432]{2,1,0:T(8,128)} %param.10) | copy-start | bytes 4435972
  17.6 0.9 copy-start.4
  18.5 0.9 copy-start.5
  19.4 94.1 %copy-start.1 = (f32[1,152,2432]{2,1,0:T(8,128)S(1)}, f32[1,152,2432]{2,1,0:T(8,128)}, u32[]{:S(2)}) copy-start(f32[1,152,2432]{2,1,0:T(8,128)} %param.10) | copy-start | bytes 4435972
Sparse Core Ops, SparseCore 0:
  10.1 78.6 all-gather.2

commit v2 on v1

--- a/solution.py
+++ b/solution.py
@@ -21,6 +21,7 @@
 
 LEFT_PLAN = (320, 80, 16)
 RIGHT_PLAN = (608, 152, 24)
+CHUNKS = tuple(slice(at, min(at + 512, DOUT)) for at in range(0, DOUT, 512))
 
 
 def split(value):
@@ -55,7 +56,7 @@
             yield other, (x * (NZ * NC) + z * NC + c, other)
 
 
-def exchange(axis, make, send_sems, recv_sems, during=None):
+def start_exchange(axis, make, send_sems, recv_sems):
     copies = []
     for index, (other, device) in enumerate(peers(axis)):
         source, target = make(other)
@@ -69,12 +70,64 @@
         )
         copy.start()
         copies.append(copy)
+    return copies
+
+
+def exchange(axis, make, send_sems, recv_sems, during=None):
+    copies = start_exchange(axis, make, send_sems, recv_sems)
     if during is not None:
         during()
     for copy in copies:
         copy.wait()
 
 
+class Ring:
+    def __init__(self, blocks, sems):
+        self.blocks, self.sems = blocks, sems
+        x, z, c, y = place()
+        self.y = y
+        line = x * (NZ * NC) + z * NC + c
+        self.device = ((line, lax.rem(y + 1, NY)), (line, lax.rem(y + NY - 1, NY)))
+        self.sent = []
+
+    def piece(self, way, steps_back, index):
+        origin = self.y + (NY - steps_back if way == 0 else steps_back)
+        half = index % 2 if way == 0 else 1 - index % 2
+        return self.blocks.at[lax.rem(origin, NY), pl.ds(half * 64, 64)]
+
+    def copy(self, way, index, piece):
+        return pltpu.make_async_remote_copy(
+            src_ref=piece,
+            dst_ref=piece,
+            send_sem=self.sems.at[0, way, index],
+            recv_sem=self.sems.at[1, way, index],
+            device_id=self.device[way],
+            device_id_type=MESH,
+        )
+
+    def send(self, index):
+        for way in range(2):
+            copy = self.copy(way, index, self.piece(way, index // 2, index))
+            copy.start()
+            self.sent.append(copy)
+
+    def receive(self, index):
+        for way in range(2):
+            self.copy(way, index, self.piece(way, index // 2 + 1, index)).wait_recv()
+
+    def pass_on(self, index):
+        self.receive(index)
+        self.send(index + 2)
+
+    def finish(self):
+        for copy in self.sent:
+            copy.wait_send()
+
+
+def window(place_on_y):
+    return pl.ds(pl.multiple_of(place_on_y * ROWS // 16 * 16, 16), SEED_PART)
+
+
 def sum_everywhere(plan, local, bufs, sems, during):
     half_rows, x_rows, z_rows = plan
     from_core, half_sum, from_x, x_sum, from_z, z_sum, from_y, gather_z, total = bufs
@@ -112,12 +165,13 @@
 
 
 def kernel(
-    step_ref, table_ref, cot_ref, act_ref, mem_ref, seed_ref,
-    ortho_ref, factor_ref,
-    gate_ref, seed_mine, seed_other, seed_all, lhs, act4, left_rows, work, inverse,
+    step_ref, table_ref, cot_hbm, act_hbm, mem_hbm, seed_ref,
+    error_ref, factor_ref,
+    cot_ref, act_ref, mem_ref, cot_all, act_all, act_mine,
+    gate_ref, seed_mine, seed_other, seed_all, lhs, act4, left_rows, work, inverse, factor_all,
     local1, core1, half1, x1, xs1, z1, zs1, y1, g1, total1,
     local2, core2, half2, x2, xs2, z2, zs2, y2, g2, total2,
-    seed_sems, sems1, sems2,
+    load_sems, seed_sems, act_sems, ring_sems, sems1, sems2,
 ):
     x, z, c, y = place()
     barrier = pltpu.get_barrier_semaphore()
@@ -126,7 +180,15 @@
         for _, device in peers(axis):
             pl.semaphore_signal(barrier, inc=1, device_id=device, device_id_type=MESH)
             count += 1
-    pl.semaphore_wait(barrier, count)
+    loads = [
+        pltpu.make_async_copy(source, target, load_sems.at[index])
+        for index, (source, target) in enumerate(
+            ((cot_hbm, cot_ref), (act_hbm, act_ref), (mem_hbm, mem_ref))
+        )
+    ]
+    for load in loads:
+        load.start()
+    ring = Ring(cot_all, ring_sems)
 
     high, low = split(seed_ref[...])
     both = jnp.concatenate([high.astype(F32), low.astype(F32)], axis=0)
@@ -134,6 +196,10 @@
     seed_mine[y] = jnp.where(c == 0, packed[0:SEED_PART], packed[SEED_SKIP:COLS])
 
     def prepare():
+        for load in loads:
+            load.wait()
+        cot_all[y] = cot_ref[...]
+        act_all[y] = act_ref[window(y), :]
         row = lax.broadcasted_iota(jnp.int32, table_ref.shape, 0)
         gate_ref[...] = jnp.sum(
             jnp.where(row == step_ref[0], table_ref[...], 0.0), axis=0, keepdims=True
@@ -152,12 +218,26 @@
         xs1[...] = jnp.zeros_like(xs1)
         xs2[...] = jnp.zeros_like(xs2)
 
+    prepare()
+    pl.semaphore_wait(barrier, count)
     exchange(
         "y", lambda o: (seed_mine.at[y], seed_mine.at[y]),
-        seed_sems.at[0, 0], seed_sems.at[1, 0], prepare,
-    )
+        seed_sems.at[0, 0], seed_sems.at[1, 0],
+    )
+    act_copies = []
+
+    def first_blocks():
+        act_copies.extend(
+            start_exchange(
+                "y", lambda o: (act_ref.at[window(o)], act_all.at[y]),
+                act_sems.at[0], act_sems.at[1],
+            )
+        )
+        ring.send(0)
+
     exchange(
-        "core", lambda o: (seed_mine, seed_other), seed_sems.at[0, 1], seed_sems.at[1, 1]
+        "core", lambda o: (seed_mine, seed_other), seed_sems.at[0, 1], seed_sems.at[1, 1],
+        first_blocks,
     )
     for block in range(NY):
         mine, other = seed_mine[block], seed_other[block]
@@ -189,8 +269,13 @@
     twice = jnp.concatenate([memory, memory], axis=1)
     local1[my_rows, :] = local1[my_rows, :] + jnp.where(lane_half == y // 4, twice, 0.0)
 
+    def later_blocks():
+        ring.pass_on(0)
+        ring.pass_on(1)
+
     sum_everywhere(
-        LEFT_PLAN, local1, (core1, half1, x1, xs1, z1, zs1, y1, g1, total1), sems1, [None] * 7
+        LEFT_PLAN, local1, (core1, half1, x1, xs1, z1, zs1, y1, g1, total1), sems1,
+        [None, lambda: ring.send(1), None, None, later_blocks, None, None],
     )
 
     left_high, left_low = split(total1[0:HALF, :])
@@ -208,8 +293,8 @@
     left_mine = jnp.where(y // 4 == 0, pair[:, 0:RANK], pair[:, RANK:128])
     mine_high, mine_low = split(left_mine)
     mine_both = jnp.concatenate([mine_high, mine_low], axis=1)
-    for first, last in ((0, 4), (4, 8), (8, 12), (12, 16), (16, 19)):
-        cols = slice(first * 128, last * 128)
+    for cols in CHUNKS:
+        first, last = cols.start // 128, cols.stop // 128
         by_token = mm(thr_both, cot_ref[:, cols])
         by_high = mm(mine_both, lhs[256 : 256 + ROWS, cols], ((0,), (0,)))
         by_low = mm(mine_high, lhs[416 : 416 + ROWS, cols], ((0,), (0,)))
@@ -250,15 +335,46 @@
         pivots = jnp.sum(jnp.where(row == lane, whole, 0.0), axis=1, keepdims=True)
         inverse[...] = whole[:, RANK:128] / jnp.sqrt(pivots)
 
+    def merge():
+        for source in range(NY):
+            rows = act_all[source]
+            act_mine[:, source * 128 : (source + 1) * 128] = jnp.where(
+                lax.rem(y, 2) == 1, rows[8:SEED_PART], rows[0:ROWS]
+            )
+        for cols in CHUNKS:
+            gradient = mm(act_mine[...], cot_all[:, :, cols].reshape(NY * 128, -1))
+            error_ref[:, cols] = gradient * gate_ref[:, cols] + mem_ref[:, cols]
+
+    def core_stage():
+        ring.pass_on(2)
+        ring.pass_on(3)
+        gram()
+
+    def z_stage():
+        eliminate(16, 24)
+        ring.pass_on(4)
+        eliminate(24, 32)
+
+    def gather_z_stage():
+        eliminate(48, 64)
+        finish()
+
+    def gather_x_stage():
+        ring.receive(5)
+        ring.receive(6)
+        for copy in act_copies:
+            copy.wait()
+        merge()
+
     sum_everywhere(
         RIGHT_PLAN, local2, (core2, half2, x2, xs2, z2, zs2, y2, g2, total2), sems2,
         [
-            gram,
+            core_stage,
             lambda: eliminate(0, 16),
-            lambda: eliminate(16, 32),
+            z_stage,
             lambda: eliminate(32, 48),
-            lambda: eliminate(48, 64),
-            finish,
+            gather_z_stage,
+            gather_x_stage,
             None,
         ],
     )
@@ -268,14 +384,35 @@
     inv_lhs = jnp.concatenate(
         [inv_high.astype(F32), inv_high.astype(F32), inv_low.astype(F32)], axis=1
     ).astype(BF16)
-    for tile in range(DOUT // 128):
-        high, low = split(total2[tile * RANK : (tile + 1) * RANK, :])
-        rhs = jnp.concatenate([high, low, high], axis=0)
-        factor_ref[:, tile * 128 : (tile + 1) * 128] = mm(inv_lhs, rhs) * (1.0 / 64)
-    ortho_ref[...] = lax.dot_general(
+    ortho = lax.dot_general(
         left_mine, inv, (((1,), (1,)), ((), ())),
         precision=lax.Precision.HIGHEST, preferred_element_type=F32,
     )
+    ort_high, ort_low = split(ortho)
+    ortho_lhs = jnp.concatenate(
+        [ort_high.astype(F32), ort_high.astype(F32), ort_low.astype(F32)], axis=1
+    ).astype(BF16)
+    for cols in CHUNKS:
+        summed = jnp.concatenate(
+            [
+                total2[tile * RANK : (tile + 1) * RANK, :]
+                for tile in range(cols.start // 128, cols.stop // 128)
+            ],
+            axis=1,
+        )
+        high, low = split(summed)
+        factor = mm(inv_lhs, jnp.concatenate([high, low, high], axis=0)) * (1.0 / 64)
+        factor_all[:, cols] = factor
+        high, low = split(factor)
+        error_ref[:, cols] = error_ref[:, cols] - mm(
+            ortho_lhs, jnp.concatenate([high, low, high], axis=0)
+        )
+    mine = jnp.zeros((RANK, COLS), F32)
+    for block in range(NY):
+        part = factor_all[:, block * COLS : (block + 1) * COLS]
+        mine = jnp.where(y == block, part, mine)
+    factor_ref[...] = mine
+    ring.finish()
 
 
 def plan_scratch(plan):
@@ -299,12 +436,20 @@
     return pl.pallas_call(
         kernel,
         out_shape=(
-            jax.ShapeDtypeStruct((ROWS, RANK), F32),
-            jax.ShapeDtypeStruct((RANK, DOUT), F32),
+            jax.ShapeDtypeStruct((ROWS, DOUT), F32),
+            jax.ShapeDtypeStruct((RANK, COLS), F32),
         ),
-        in_specs=[pl.BlockSpec(memory_space=pltpu.SMEM)] + [vmem] * 5,
+        in_specs=[pl.BlockSpec(memory_space=pltpu.SMEM), vmem]
+        + [pl.BlockSpec(memory_space=pl.ANY)] * 3
+        + [vmem],
         out_specs=(vmem, vmem),
         scratch_shapes=[
+            pltpu.VMEM((128, DOUT), BF16),
+            pltpu.VMEM((DIN, 128), BF16),
+            pltpu.VMEM((ROWS, DOUT), F32),
+            pltpu.VMEM((NY, 128, DOUT), BF16),
+            pltpu.VMEM((NY, SEED_PART, 128), BF16),
+            pltpu.VMEM((ROWS, NY * 128), BF16),
             pltpu.VMEM((1, DOUT), F32),
             pltpu.VMEM((NY, SEED_PART, 128), BF16),
             pltpu.VMEM((NY, SEED_PART, 128), BF16),
@@ -314,38 +459,29 @@
             pltpu.VMEM((DIN, 128), BF16),
             pltpu.VMEM((RANK, 128), F32),
             pltpu.VMEM((RANK, RANK), F32),
+            pltpu.VMEM((RANK, DOUT), F32),
         ]
         + plan_scratch(LEFT_PLAN)
         + plan_scratch(RIGHT_PLAN)
         + [
+            pltpu.SemaphoreType.DMA((3,)),
+            pltpu.SemaphoreType.DMA((2, 2, 7)),
+            pltpu.SemaphoreType.DMA((2, 7)),
             pltpu.SemaphoreType.DMA((2, 2, 7)),
             pltpu.SemaphoreType.DMA((2, 7, 7)),
             pltpu.SemaphoreType.DMA((2, 7, 7)),
         ],
         compiler_params=pltpu.CompilerParams(
-            collective_id=0, has_side_effects=True, vmem_limit_bytes=48 * 2**20
+            collective_id=0, has_side_effects=True, vmem_limit_bytes=60 * 2**20
         ),
     )(timesteps, gate_table, cot, act_t, memory, seed_t)
 
 
 def per_device(activations, cotangent, timesteps, gate_table, error_in, seed_factor):
-    act_rows = activations[0]
-    cot_rows = cotangent[0]
-    memory = error_in[0]
-    step_ids = jnp.arange(gate_table.shape[0], dtype=jnp.int32)
-    gate_row = jnp.sum(jnp.where(step_ids[:, None] == timesteps[0], gate_table, 0.0), 0)
-    columns = lax.all_to_all(act_rows, "seq", split_axis=1, concat_axis=0, tiled=True)
-    cot_all = lax.all_gather(cot_rows, "seq", axis=0, tiled=True)
-    ortho, factor_t = factors(
-        timesteps, gate_table, cot_rows, act_rows.T, memory, seed_factor.T
-    )
-    gradient = mm(columns, cot_all, ((0,), (0,)))
-    merged = gradient * gate_row + memory
-    error_out = merged - jnp.dot(ortho, factor_t, precision=lax.Precision.HIGHEST)
-    factor_mine = lax.dynamic_slice_in_dim(
-        factor_t, lax.axis_index("seq") * COLS, COLS, 1
-    ).T
-    return error_out[None], factor_mine
+    error_out, factor_t = factors(
+        timesteps, gate_table, cotangent[0], activations[0].T, error_in[0], seed_factor.T
+    )
+    return error_out[None], factor_t.T
 
 
 def solution(mesh):

time: 127 us -> 110 us (0.87)
  between operations: 14.8 us -> 1.29 us
  Pallas kernels: 93.2 us -> 105 us
  starting transfers between devices: 7.7 us -> 0 us
  matrix products: 5.96 us -> 0 us
    pallas_call x1, Pallas kernels: 93.2 us -> 105 us  [factors(): pl.pallas_call(kernel, out_shape=(jax.ShapeDtypeStruct((ROWS, DOUT), F32)...]
    all_to_all x1 -> x0, starting transfers between devices: 7.66 us -> none  [per_device(): lax.all_to_all(act_rows, 'seq', split_axis=1, concat_axis=0, tiled=True)]
    dot_general x2 -> x0, matrix products: 5.96 us -> none  [the longest x1 3.44 us: mm(): lax.dot_general(first, second, (dims, ((), ())), preferred_element_type=F32)]
    unnamed x12 -> x4, local copies, waits for them, and re-layouts: 3.19 us -> 3.26 us
  transfers between devices with their start and end apart: 2 -> 0, of which waited for: 0 -> 0; matrix products, arithmetic and copies ran while one was open for 1% -> 0% of each run, Pallas kernels for 74% -> 0%
where the time goes in v2:
time: 110 us; the launch traced here: 109 us
  Pallas kernels  105 us (95%)
  local copies, waits for them, and re-layouts  3.26 us (3%)
  between operations  1.29 us (1%)
    pallas_call x1, Pallas kernels, factors(): pl.pallas_call(kernel, out_shape=(jax.ShapeDtypeStruct((ROWS, DOUT), F32)...  105 us
    unnamed x4, local copies, waits for them, and re-layouts  3.26 us

profile of v2, /device:TPU:1, one launch (start us, length us, event | category | flops | bytes accessed | tf_op | source)
XLA Modules:
  0.0 109.5 jit_solution(2864706350618482431)
XLA Ops:
  1.3 104.9 %shard_map.77 = (f32[152,2432]{1,0:T(8,128)}, f32[64,304]{1,0:T(8,128)}) custom-call(s32[1]{0:T(128)S(6)} %copy.10.step_ref, f32[16,2432]{1,0:T(8,128)} %table_ref.1, bf16[128,2432]{1,0:T(8,128)(2,1)} %bitcast.10, bf16[1216,128]{1,0:T(8,128)(2,1)} %bitcast.11, f32[152,2432]{1,0:T(8,128)} %bitcast.8, f32[64,304]{1,0:T(8,128)} %bitcast.12), custom_call_target="tpu_custom_call" | custom-call | tf_op jit(solution)/shard_map/pallas_call | solution.py:436
  106.2 0.0 copy-start
  106.2 2.6 %copy.11 = f32[1,152,2432]{2,1,0:T(8,128)} copy(f32[1,152,2432]{2,1,0:T(8,128)} %bitcast.9) | data formatting | bytes 2957312
  108.9 0.0 copy-done
  108.9 0.6 copy.12
Async XLA Ops:
  106.2 2.6 %copy-start = (f32[64,304]{1,0:T(8,128)S(1)}, f32[64,304]{1,0:T(8,128)}, u32[]{:S(2)}) copy-start(f32[64,304]{1,0:T(8,128)} %get-tuple-element.5) | copy-start | bytes 233476

commit v3 on v2

--- a/solution.py
+++ b/solution.py
@@ -195,11 +195,20 @@
     packed = both.T.astype(BF16)
     seed_mine[y] = jnp.where(c == 0, packed[0:SEED_PART], packed[SEED_SKIP:COLS])
 
+    for load in loads:
+        load.wait()
+    cot_all[y] = cot_ref[...]
+    act_all[y] = act_ref[window(y), :]
+    act_copies = []
+
     def prepare():
-        for load in loads:
-            load.wait()
-        cot_all[y] = cot_ref[...]
-        act_all[y] = act_ref[window(y), :]
+        act_copies.extend(
+            start_exchange(
+                "y", lambda o: (act_ref.at[window(o)], act_all.at[y]),
+                act_sems.at[0], act_sems.at[1],
+            )
+        )
+        ring.send(0)
         row = lax.broadcasted_iota(jnp.int32, table_ref.shape, 0)
         gate_ref[...] = jnp.sum(
             jnp.where(row == step_ref[0], table_ref[...], 0.0), axis=0, keepdims=True
@@ -218,26 +227,13 @@
         xs1[...] = jnp.zeros_like(xs1)
         xs2[...] = jnp.zeros_like(xs2)
 
-    prepare()
     pl.semaphore_wait(barrier, count)
     exchange(
         "y", lambda o: (seed_mine.at[y], seed_mine.at[y]),
-        seed_sems.at[0, 0], seed_sems.at[1, 0],
-    )
-    act_copies = []
-
-    def first_blocks():
-        act_copies.extend(
-            start_exchange(
-                "y", lambda o: (act_ref.at[window(o)], act_all.at[y]),
-                act_sems.at[0], act_sems.at[1],
-            )
-        )
-        ring.send(0)
-
+        seed_sems.at[0, 0], seed_sems.at[1, 0], prepare,
+    )
     exchange(
-        "core", lambda o: (seed_mine, seed_other), seed_sems.at[0, 1], seed_sems.at[1, 1],
-        first_blocks,
+        "core", lambda o: (seed_mine, seed_other), seed_sems.at[0, 1], seed_sems.at[1, 1]
     )
     for block in range(NY):
         mine, other = seed_mine[block], seed_other[block]
@@ -270,12 +266,12 @@
     local1[my_rows, :] = local1[my_rows, :] + jnp.where(lane_half == y // 4, twice, 0.0)
 
     def later_blocks():
+        ring.send(1)
         ring.pass_on(0)
-        ring.pass_on(1)
 
     sum_everywhere(
         LEFT_PLAN, local1, (core1, half1, x1, xs1, z1, zs1, y1, g1, total1), sems1,
-        [None, lambda: ring.send(1), None, None, later_blocks, None, None],
+        [None, None, None, None, later_blocks, lambda: ring.pass_on(1), None],
     )
 
     left_high, left_low = split(total1[0:HALF, :])
@@ -347,24 +343,20 @@
 
     def core_stage():
         ring.pass_on(2)
+        gram()
+
+    def z_stage():
+        eliminate(16, 32)
+
+    def gather_z_stage():
         ring.pass_on(3)
-        gram()
-
-    def z_stage():
-        eliminate(16, 24)
         ring.pass_on(4)
-        eliminate(24, 32)
-
-    def gather_z_stage():
         eliminate(48, 64)
         finish()
 
     def gather_x_stage():
-        ring.receive(5)
-        ring.receive(6)
         for copy in act_copies:
             copy.wait()
-        merge()
 
     sum_everywhere(
         RIGHT_PLAN, local2, (core2, half2, x2, xs2, z2, zs2, y2, g2, total2), sems2,
@@ -379,6 +371,9 @@
         ],
     )
 
+    ring.receive(5)
+    ring.receive(6)
+    merge()
     inv = inverse[...]
     inv_high, inv_low = split(inv)
     inv_lhs = jnp.concatenate(

time: 110 us -> 101 us (0.918)
  Pallas kernels: 105 us -> 96.7 us
    pallas_call x1, Pallas kernels: 105 us -> 96.7 us  [factors(): pl.pallas_call(kernel, out_shape=(jax.ShapeDtypeStruct((ROWS, DOUT), F32)...]
where the time goes in v3:
time: 101 us
  Pallas kernels  96.7 us (96%)
  local copies, waits for them, and re-layouts  3.26 us (3%)
  between operations  1.29 us (1%)
    pallas_call x1, Pallas kernels, factors(): pl.pallas_call(kernel, out_shape=(jax.ShapeDtypeStruct((ROWS, DOUT), F32)...  96.7 us
    unnamed x4, local copies, waits for them, and re-layouts  3.26 us

profile of v3, /device:TPU:1, one launch (start us, length us, event | category | flops | bytes accessed | tf_op | source)
XLA Modules:
  0.0 101.3 jit_solution(14352581001986869092)
XLA Ops:
  1.3 96.7 %shard_map.77 = (f32[152,2432]{1,0:T(8,128)}, f32[64,304]{1,0:T(8,128)}) custom-call(s32[1]{0:T(128)S(6)} %copy.10.step_ref, f32[16,2432]{1,0:T(8,128)} %table_ref.1, bf16[128,2432]{1,0:T(8,128)(2,1)} %bitcast.10, bf16[1216,128]{1,0:T(8,128)(2,1)} %bitcast.11, f32[152,2432]{1,0:T(8,128)} %bitcast.8, f32[64,304]{1,0:T(8,128)} %bitcast.12), custom_call_target="tpu_custom_call" | custom-call | tf_op jit(solution)/shard_map/pallas_call | solution.py:431
  98.0 0.0 copy-start
  98.0 2.6 %copy.11 = f32[1,152,2432]{2,1,0:T(8,128)} copy(f32[1,152,2432]{2,1,0:T(8,128)} %bitcast.9) | data formatting | bytes 2957312
  100.6 0.0 copy-done
  100.6 0.6 copy.12
Async XLA Ops:
  98.0 2.6 %copy-start = (f32[64,304]{1,0:T(8,128)S(1)}, f32[64,304]{1,0:T(8,128)}, u32[]{:S(2)}) copy-start(f32[64,304]{1,0:T(8,128)} %get-tuple-element.5) | copy-start | bytes 233476

commit v4 on v2

--- a/solution.py
+++ b/solution.py
@@ -166,7 +166,7 @@
 
 def kernel(
     step_ref, table_ref, cot_hbm, act_hbm, mem_hbm, seed_ref,
-    error_ref, factor_ref,
+    error_ref, ortho_ref, parts_ref, factor_ref,
     cot_ref, act_ref, mem_ref, cot_all, act_all, act_mine,
     gate_ref, seed_mine, seed_other, seed_all, lhs, act4, left_rows, work, inverse, factor_all,
     local1, core1, half1, x1, xs1, z1, zs1, y1, g1, total1,
@@ -180,11 +180,18 @@
         for _, device in peers(axis):
             pl.semaphore_signal(barrier, inc=1, device_id=device, device_id_type=MESH)
             count += 1
+    parts = [
+        (source.at[pl.ds(at, step)], target.at[pl.ds(at, step)])
+        for source, target, step in (
+            (act_hbm, act_ref, 304), (cot_hbm, cot_ref, 32), (mem_hbm, mem_ref, 24),
+        )
+        for at in range(0, source.shape[0] // step * step, step)
+    ]
+    last = pl.ds(ROWS // 24 * 24, ROWS % 24)
+    parts.append((mem_hbm.at[last], mem_ref.at[last]))
     loads = [
         pltpu.make_async_copy(source, target, load_sems.at[index])
-        for index, (source, target) in enumerate(
-            ((cot_hbm, cot_ref), (act_hbm, act_ref), (mem_hbm, mem_ref))
-        )
+        for index, (source, target) in enumerate(parts)
     ]
     for load in loads:
         load.start()
@@ -194,6 +201,8 @@
     both = jnp.concatenate([high.astype(F32), low.astype(F32)], axis=0)
     packed = both.T.astype(BF16)
     seed_mine[y] = jnp.where(c == 0, packed[0:SEED_PART], packed[SEED_SKIP:COLS])
+
+    act_copies = []
 
     def prepare():
         for load in loads:
@@ -218,14 +227,7 @@
         xs1[...] = jnp.zeros_like(xs1)
         xs2[...] = jnp.zeros_like(xs2)
 
-    prepare()
     pl.semaphore_wait(barrier, count)
-    exchange(
-        "y", lambda o: (seed_mine.at[y], seed_mine.at[y]),
-        seed_sems.at[0, 0], seed_sems.at[1, 0],
-    )
-    act_copies = []
-
     def first_blocks():
         act_copies.extend(
             start_exchange(
@@ -235,10 +237,31 @@
         )
         ring.send(0)
 
-    exchange(
-        "core", lambda o: (seed_mine, seed_other), seed_sems.at[0, 1], seed_sems.at[1, 1],
-        first_blocks,
-    )
+    def to_sibling(block, index):
+        (_, device), = peers("core")
+        copy = pltpu.make_async_remote_copy(
+            src_ref=seed_mine.at[block],
+            dst_ref=seed_other.at[block],
+            send_sem=seed_sems.at[0, 1, index],
+            recv_sem=seed_sems.at[1, 1, index],
+            device_id=device,
+            device_id_type=MESH,
+        )
+        copy.start()
+        return copy
+
+    along_y = start_exchange(
+        "y", lambda o: (seed_mine.at[y], seed_mine.at[y]),
+        seed_sems.at[0, 0], seed_sems.at[1, 0],
+    )
+    swaps = [to_sibling(y, 0)]
+    prepare()
+    for step in (1, 7, 2, 6, 3, 5, 4):
+        along_y[step - 1].wait()
+        swaps.append(to_sibling(lax.rem(y + NY - step, NY), step))
+    first_blocks()
+    for copy in swaps:
+        copy.wait()
     for block in range(NY):
         mine, other = seed_mine[block], seed_other[block]
         start = block * COLS
@@ -270,12 +293,12 @@
     local1[my_rows, :] = local1[my_rows, :] + jnp.where(lane_half == y // 4, twice, 0.0)
 
     def later_blocks():
+        ring.send(1)
         ring.pass_on(0)
-        ring.pass_on(1)
 
     sum_everywhere(
         LEFT_PLAN, local1, (core1, half1, x1, xs1, z1, zs1, y1, g1, total1), sems1,
-        [None, lambda: ring.send(1), None, None, later_blocks, None, None],
+        [None, None, None, later_blocks, lambda: ring.pass_on(1), None, None],
     )
 
     left_high, left_low = split(total1[0:HALF, :])
@@ -347,35 +370,29 @@
 
     def core_stage():
         ring.pass_on(2)
+        gram()
+
+    def y_stage():
         ring.pass_on(3)
-        gram()
-
-    def z_stage():
-        eliminate(16, 24)
         ring.pass_on(4)
-        eliminate(24, 32)
-
-    def gather_z_stage():
-        eliminate(48, 64)
-        finish()
+        eliminate(32, 64)
 
     def gather_x_stage():
+        for copy in act_copies:
+            copy.wait()
         ring.receive(5)
         ring.receive(6)
-        for copy in act_copies:
-            copy.wait()
-        merge()
 
     sum_everywhere(
         RIGHT_PLAN, local2, (core2, half2, x2, xs2, z2, zs2, y2, g2, total2), sems2,
         [
             core_stage,
             lambda: eliminate(0, 16),
-            z_stage,
-            lambda: eliminate(32, 48),
-            gather_z_stage,
+            lambda: eliminate(16, 32),
+            y_stage,
+            finish,
             gather_x_stage,
-            None,
+            merge,
         ],
     )
 
@@ -389,7 +406,7 @@
         precision=lax.Precision.HIGHEST, preferred_element_type=F32,
     )
     ort_high, ort_low = split(ortho)
-    ortho_lhs = jnp.concatenate(
+    ortho_ref[...] = jnp.concatenate(
         [ort_high.astype(F32), ort_high.astype(F32), ort_low.astype(F32)], axis=1
     ).astype(BF16)
     for cols in CHUNKS:
@@ -404,9 +421,7 @@
         factor = mm(inv_lhs, jnp.concatenate([high, low, high], axis=0)) * (1.0 / 64)
         factor_all[:, cols] = factor
         high, low = split(factor)
-        error_ref[:, cols] = error_ref[:, cols] - mm(
-            ortho_lhs, jnp.concatenate([high, low, high], axis=0)
-        )
+        parts_ref[:, cols] = jnp.concatenate([high, low, high], axis=0)
     mine = jnp.zeros((RANK, COLS), F32)
     for block in range(NY):
         part = factor_all[:, block * COLS : (block + 1) * COLS]
@@ -436,13 +451,15 @@
     return pl.pallas_call(
         kernel,
         out_shape=(
-            jax.ShapeDtypeStruct((ROWS, DOUT), F32),
-            jax.ShapeDtypeStruct((RANK, COLS), F32),
+            pltpu.VMEM((ROWS, DOUT), F32),
+            pltpu.VMEM((ROWS, 3 * RANK), BF16),
+            pltpu.VMEM((3 * RANK, DOUT), BF16),
+            pltpu.VMEM((RANK, COLS), F32),
         ),
         in_specs=[pl.BlockSpec(memory_space=pltpu.SMEM), vmem]
-        + [pl.BlockSpec(memory_space=pl.ANY)] * 3
+        + [pl.BlockSpec(memory_space=pltpu.HBM)] * 3
         + [vmem],
-        out_specs=(vmem, vmem),
+        out_specs=(vmem,) * 4,
         scratch_shapes=[
             pltpu.VMEM((128, DOUT), BF16),
             pltpu.VMEM((DIN, 128), BF16),
@@ -464,8 +481,8 @@
         + plan_scratch(LEFT_PLAN)
         + plan_scratch(RIGHT_PLAN)
         + [
-            pltpu.SemaphoreType.DMA((3,)),
-            pltpu.SemaphoreType.DMA((2, 2, 7)),
+            pltpu.SemaphoreType.DMA((16,)),
+            pltpu.SemaphoreType.DMA((2, 2, 8)),
             pltpu.SemaphoreType.DMA((2, 7)),
             pltpu.SemaphoreType.DMA((2, 2, 7)),
             pltpu.SemaphoreType.DMA((2, 7, 7)),
@@ -477,9 +494,45 @@
     )(timesteps, gate_table, cot, act_t, memory, seed_t)
 
 
+def store_kernel(
+    merged_ref, ortho_ref, parts_ref, factor_ref, error_out, factor_out, error_ref, sems
+):
+    copies = [pltpu.make_async_copy(factor_ref, factor_out, sems.at[0])]
+    copies[0].start()
+    for index, cols in enumerate(CHUNKS):
+        error_ref[:, cols] = merged_ref[:, cols] - mm(ortho_ref[...], parts_ref[:, cols])
+        copies.append(
+            pltpu.make_async_copy(
+                error_ref.at[:, cols], error_out.at[:, cols], sems.at[index + 1]
+            )
+        )
+        copies[-1].start()
+    for copy in copies:
+        copy.wait()
+
+
+def store(merged, ortho, parts, factor):
+    return pl.pallas_call(
+        store_kernel,
+        out_shape=(
+            jax.ShapeDtypeStruct(merged.shape, F32),
+            jax.ShapeDtypeStruct(factor.shape, F32),
+        ),
+        in_specs=[pl.BlockSpec(memory_space=pltpu.VMEM)] * 4,
+        out_specs=(pl.BlockSpec(memory_space=pltpu.HBM),) * 2,
+        scratch_shapes=[
+            pltpu.VMEM((ROWS, DOUT), F32),
+            pltpu.SemaphoreType.DMA((1 + len(CHUNKS),)),
+        ],
+        compiler_params=pltpu.CompilerParams(vmem_limit_bytes=16 * 2**20),
+    )(merged, ortho, parts, factor)
+
+
 def per_device(activations, cotangent, timesteps, gate_table, error_in, seed_factor):
-    error_out, factor_t = factors(
-        timesteps, gate_table, cotangent[0], activations[0].T, error_in[0], seed_factor.T
+    error_out, factor_t = store(
+        *factors(
+            timesteps, gate_table, cotangent[0], activations[0].T, error_in[0], seed_factor.T
+        )
     )
     return error_out[None], factor_t.T
 

time: 110 us -> 94.4 us (0.86)
  Pallas kernels: 105 us -> 93 us
  local copies, waits for them, and re-layouts: 3.26 us -> 0 us
    pallas_call x1 -> x2, Pallas kernels: 105 us -> 93 us  [the longest x1 91.6 us: factors(): pl.pallas_call(kernel, out_shape=(pltpu.VMEM((ROWS, DOUT), F32), pltpu.VM...]
    unnamed x4 -> x0, local copies, waits for them, and re-layouts: 3.26 us -> none
where the time goes in v4:
time: 94.4 us; the launch traced here: 94.2 us
  Pallas kernels  93 us (99%)
  between operations  1.28 us (1%)
    pallas_call x1, Pallas kernels, factors(): pl.pallas_call(kernel, out_shape=(pltpu.VMEM((ROWS, DOUT), F32), pltpu.VM...  91.6 us

profile of v4, /device:TPU:1, one launch (start us, length us, event | category | flops | bytes accessed | tf_op | source)
XLA Modules:
  0.0 94.2 jit_solution(1251973876001841522)
XLA Ops:
  1.3 91.6 %shard_map.77 = (f32[152,2432]{1,0:T(8,128)S(1)}, bf16[152,192]{1,0:T(8,128)(2,1)S(1)}, bf16[192,2432]{1,0:T(8,128)(2,1)S(1)}, f32[64,304]{1,0:T(8,128)S(1)}) custom-call(s32[1]{0:T(128)S(6)} %copy.8.step_ref, f32[16,2432]{1,0:T(8,128)} %table_ref.1, bf16[128,2432]{1,0:T(8,128)(2,1)} %bitcast.9, bf16[1216,128]{1,0:T(8,128)(2,1)} %bitcast.10, ...), custom_call_target="tpu_custom_call" | custom-call | tf_op jit(solution)/shard_map/pallas_call | solution.py:451
  92.9 1.4 %shard_map.78 = (f32[152,2432]{1,0:T(8,128)}, f32[64,304]{1,0:T(8,128)}) custom-call(f32[152,2432]{1,0:T(8,128)S(1)} %get-tuple-element.8.merged_ref, bf16[152,192]{1,0:T(8,128)(2,1)S(1)} %get-tuple-element.9.ortho_ref, bf16[192,2432]{1,0:T(8,128)(2,1)S(1)} %get-tuple-element.10.parts_ref, f32[64,304]{1,0:T(8,128)S(1)} %get-tuple-element.11.factor_ref), custom_call_target="tpu_custom_call" | custom-call | tf_op jit(solution)/shard_map/pallas_call | solution.py:515

commit v5 on v4

--- a/solution.py
+++ b/solution.py
@@ -130,38 +130,127 @@
 
 def sum_everywhere(plan, local, bufs, sems, during):
     half_rows, x_rows, z_rows = plan
-    from_core, half_sum, from_x, x_sum, from_z, z_sum, from_y, gather_z, total = bufs
+    used = -(-x_rows // z_rows)
+    from_core, from_x, x_sum, from_z, z_sum, from_y, gathered, total = bufs
     x, z, c, y = place()
-
-    def sem(stage):
-        return sems.at[0, stage], sems.at[1, stage]
+    (_, sibling), = peers("core")
+    x_peers, z_peers = list(peers("x")), list(peers("z"))
 
     def part(index, rows):
         return pl.ds(pl.multiple_of(index * rows, 8), rows)
 
-    exchange("core", lambda o: (local.at[part(o, half_rows)], from_core), *sem(0), during[0])
-    half_sum[...] = local[part(c, half_rows), :] + from_core[...]
-
-    exchange("x", lambda o: (half_sum.at[part(o, x_rows)], from_x.at[x]), *sem(1), during[1])
-    from_x[x] = half_sum[part(x, x_rows), :]
+    def remote(stage, index, source, target, device):
+        return pltpu.make_async_remote_copy(
+            src_ref=source,
+            dst_ref=target,
+            send_sem=sems.at[0, stage, index],
+            recv_sem=sems.at[1, stage, index],
+            device_id=device,
+            device_id_type=MESH,
+        )
+
+    def beside(stage):
+        if during[stage] is not None:
+            during[stage]()
+
+    places = [other for other, _ in x_peers] + [x]
+    copies = []
+    for index, other in enumerate(places):
+        mine = part((1 - c) * NX + other, x_rows)
+        copies.append(
+            remote(0, index, local.at[mine], from_core.at[part(other, x_rows)], sibling)
+        )
+        copies[-1].start()
+    beside(0)
+    x_copies = []
+    for index, other in enumerate(places):
+        copies[index].wait()
+        rows = part(other, x_rows)
+        both = local[part(c * NX + other, x_rows), :] + from_core[rows, :]
+        if index < NX - 1:
+            from_core[rows, :] = both
+            x_copies.append(
+                remote(1, index, from_core.at[rows], from_x.at[x], x_peers[index][1])
+            )
+            x_copies[-1].start()
+        else:
+            from_x[x] = both
+    beside(1)
+    for copy in x_copies:
+        copy.wait()
     x_sum[0:x_rows, :] = (from_x[0] + from_x[1]) + (from_x[2] + from_x[3])
 
-    exchange("z", lambda o: (x_sum.at[part(o, z_rows)], from_z.at[z]), *sem(2), during[2])
+    copies = start_exchange(
+        "z", lambda o: (x_sum.at[part(o, z_rows)], from_z.at[z]), sems.at[0, 2], sems.at[1, 2]
+    )
     from_z[z] = x_sum[part(z, z_rows), :]
+    beside(2)
+    for copy in copies:
+        copy.wait()
     z_sum[...] = jnp.sum(from_z[...], axis=0)
 
-    exchange("y", lambda o: (z_sum, from_y.at[y]), *sem(3), during[3])
+    copies = start_exchange("y", lambda o: (z_sum, from_y.at[y]), sems.at[0, 3], sems.at[1, 3])
     from_y[y] = z_sum[...]
-    gather_z[z] = jnp.sum(from_y[...], axis=0)
-
-    exchange("z", lambda o: (gather_z.at[z], gather_z.at[z]), *sem(4), during[4])
-    total[part(c * NX + x, x_rows), :] = gather_z[...].reshape(NZ * z_rows, 128)[0:x_rows]
-
-    mine = total.at[part(c * NX + x, x_rows)]
-    exchange("x", lambda o: (mine, mine), *sem(5), during[5])
-
-    mine_half = total.at[part(c, half_rows)]
-    exchange("core", lambda o: (mine_half, mine_half), *sem(6), during[6])
+    beside(3)
+    for copy in copies:
+        copy.wait()
+    gathered[c, x, z] = jnp.sum(from_y[...], axis=0)
+
+    def forward(step):
+        piece = lax.rem(z + NZ - step, NZ)
+        ref = gathered.at[c, x, piece]
+        return piece < used, [
+            remote(5 + index, piece, ref, ref, device)
+            for index, (_, device) in enumerate(x_peers)
+        ]
+
+    def start_forward(step):
+        wanted, forwards = forward(step)
+
+        @pl.when(wanted)
+        def _():
+            for copy in forwards:
+                copy.start()
+
+    own = gathered.at[c, x, z]
+    copies = start_exchange("z", lambda o: (own, own), sems.at[0, 4], sems.at[1, 4])
+    start_forward(0)
+    beside(4)
+    for step in (1, 7, 2, 6, 3, 5, 4):
+        copies[step - 1].wait()
+        start_forward(step)
+
+    def to_sibling(index, other):
+        ref = gathered.at[c, other, pl.ds(0, used)]
+        copy = remote(8, index, ref, ref, sibling)
+        copy.start()
+        return copy
+
+    copies = [to_sibling(0, x)]
+    beside(5)
+    for index in (0, 2, 1):
+        other = lax.rem(x + NX - 1 - index, NX)
+        for piece in range(used):
+            ref = gathered.at[c, other, piece]
+            remote(5 + index, piece, ref, ref, x_peers[index][1]).wait_recv()
+        copies.append(to_sibling(1 + index, other))
+    beside(6)
+    for copy in copies:
+        copy.wait()
+    for step in range(NZ):
+        wanted, forwards = forward(step)
+
+        @pl.when(wanted)
+        def _():
+            for copy in forwards:
+                copy.wait_send()
+
+    for core in range(NC):
+        for at in range(NX):
+            first = (core * NX + at) * x_rows
+            total[first : first + x_rows, :] = (
+                gathered[core, at].reshape(NZ * z_rows, 128)[0:x_rows]
+            )
 
 
 def kernel(
@@ -169,8 +258,8 @@
     error_ref, ortho_ref, parts_ref, factor_ref,
     cot_ref, act_ref, mem_ref, cot_all, act_all, act_mine,
     gate_ref, seed_mine, seed_other, seed_all, lhs, act4, left_rows, work, inverse, factor_all,
-    local1, core1, half1, x1, xs1, z1, zs1, y1, g1, total1,
-    local2, core2, half2, x2, xs2, z2, zs2, y2, g2, total2,
+    local1, core1, x1, xs1, z1, zs1, y1, g1, total1,
+    local2, core2, x2, xs2, z2, zs2, y2, g2, total2,
     load_sems, seed_sems, act_sems, ring_sems, sems1, sems2,
 ):
     x, z, c, y = place()
@@ -297,8 +386,8 @@
         ring.pass_on(0)
 
     sum_everywhere(
-        LEFT_PLAN, local1, (core1, half1, x1, xs1, z1, zs1, y1, g1, total1), sems1,
-        [None, None, None, later_blocks, lambda: ring.pass_on(1), None, None],
+        LEFT_PLAN, local1, (core1, x1, xs1, z1, zs1, y1, g1, total1), sems1,
+        [None, None, None, later_blocks, None, lambda: ring.pass_on(1), None],
     )
 
     left_high, left_low = split(total1[0:HALF, :])
@@ -377,22 +466,23 @@
         ring.pass_on(4)
         eliminate(32, 64)
 
-    def gather_x_stage():
+    def last_stage():
         for copy in act_copies:
             copy.wait()
         ring.receive(5)
         ring.receive(6)
+        merge()
 
     sum_everywhere(
-        RIGHT_PLAN, local2, (core2, half2, x2, xs2, z2, zs2, y2, g2, total2), sems2,
+        RIGHT_PLAN, local2, (core2, x2, xs2, z2, zs2, y2, g2, total2), sems2,
         [
             core_stage,
             lambda: eliminate(0, 16),
             lambda: eliminate(16, 32),
             y_stage,
             finish,
-            gather_x_stage,
-            merge,
+            None,
+            last_stage,
         ],
     )
 
@@ -435,13 +525,12 @@
     return [
         pltpu.VMEM((2 * half_rows, 128), F32),
         pltpu.VMEM((half_rows, 128), F32),
-        pltpu.VMEM((half_rows, 128), F32),
         pltpu.VMEM((NX, x_rows, 128), F32),
         pltpu.VMEM((NZ * z_rows, 128), F32),
         pltpu.VMEM((NZ, z_rows, 128), F32),
         pltpu.VMEM((z_rows, 128), F32),
         pltpu.VMEM((NY, z_rows, 128), F32),
-        pltpu.VMEM((NZ, z_rows, 128), F32),
+        pltpu.VMEM((NC, NX, NZ, z_rows, 128), F32),
         pltpu.VMEM((2 * half_rows, 128), F32),
     ]
 
@@ -485,8 +574,8 @@
             pltpu.SemaphoreType.DMA((2, 2, 8)),
             pltpu.SemaphoreType.DMA((2, 7)),
             pltpu.SemaphoreType.DMA((2, 2, 7)),
-            pltpu.SemaphoreType.DMA((2, 7, 7)),
-            pltpu.SemaphoreType.DMA((2, 7, 7)),
+            pltpu.SemaphoreType.DMA((2, 9, 8)),
+            pltpu.SemaphoreType.DMA((2, 9, 8)),
         ],
         compiler_params=pltpu.CompilerParams(
             collective_id=0, has_side_effects=True, vmem_limit_bytes=60 * 2**20

time: 94.4 us -> 92.4 us (0.979)
  Pallas kernels: 93 us -> 91 us
    pallas_call x1, Pallas kernels: 91.6 us -> 89.6 us  [factors(): pl.pallas_call(kernel, out_shape=(pltpu.VMEM((ROWS, DOUT), F32), pltpu.VM...]
where the time goes in v5:
time: 92.4 us; the launch traced here: 92.2 us
  Pallas kernels  91 us (98%)
  between operations  1.28 us (1%)
    pallas_call x1, Pallas kernels, factors(): pl.pallas_call(kernel, out_shape=(pltpu.VMEM((ROWS, DOUT), F32), pltpu.VM...  89.6 us

profile of v5, /device:TPU:1, one launch (start us, length us, event | category | flops | bytes accessed | tf_op | source)
XLA Modules:
  0.0 92.2 jit_solution(3361022354059526560)
XLA Ops:
  1.3 89.6 %shard_map.77 = (f32[152,2432]{1,0:T(8,128)S(1)}, bf16[152,192]{1,0:T(8,128)(2,1)S(1)}, bf16[192,2432]{1,0:T(8,128)(2,1)S(1)}, f32[64,304]{1,0:T(8,128)S(1)}) custom-call(s32[1]{0:T(128)S(6)} %copy.8.step_ref, f32[16,2432]{1,0:T(8,128)} %table_ref.1, bf16[128,2432]{1,0:T(8,128)(2,1)} %bitcast.9, bf16[1216,128]{1,0:T(8,128)(2,1)} %bitcast.10, ...), custom_call_target="tpu_custom_call" | custom-call | tf_op jit(solution)/shard_map/pallas_call | solution.py:540
  90.9 1.4 %shard_map.78 = (f32[152,2432]{1,0:T(8,128)}, f32[64,304]{1,0:T(8,128)}) custom-call(f32[152,2432]{1,0:T(8,128)S(1)} %get-tuple-element.8.merged_ref, bf16[152,192]{1,0:T(8,128)(2,1)S(1)} %get-tuple-element.9.ortho_ref, bf16[192,2432]{1,0:T(8,128)(2,1)S(1)} %get-tuple-element.10.parts_ref, f32[64,304]{1,0:T(8,128)S(1)} %get-tuple-element.11.factor_ref), custom_call_target="tpu_custom_call" | custom-call | tf_op jit(solution)/shard_map/pallas_call | solution.py:604

commit v6 on v5

--- a/solution.py
+++ b/solution.py
@@ -254,9 +254,9 @@
 
 
 def kernel(
-    step_ref, table_ref, cot_hbm, act_hbm, mem_hbm, seed_ref,
+    step_hbm, table_hbm, cot_hbm, act_hbm, mem_hbm, seed_hbm,
     error_ref, ortho_ref, parts_ref, factor_ref,
-    cot_ref, act_ref, mem_ref, cot_all, act_all, act_mine,
+    step_ref, table_ref, seed_ref, cot_ref, act_ref, mem_ref, cot_all, act_all, act_mine,
     gate_ref, seed_mine, seed_other, seed_all, lhs, act4, left_rows, work, inverse, factor_all,
     local1, core1, x1, xs1, z1, zs1, y1, g1, total1,
     local2, core2, x2, xs2, z2, zs2, y2, g2, total2,
@@ -269,7 +269,9 @@
         for _, device in peers(axis):
             pl.semaphore_signal(barrier, inc=1, device_id=device, device_id_type=MESH)
             count += 1
-    parts = [
+    seed_load = pltpu.make_async_copy(seed_hbm, seed_ref, load_sems.at[17])
+    seed_load.start()
+    parts = [(step_hbm, step_ref), (table_hbm, table_ref)] + [
         (source.at[pl.ds(at, step)], target.at[pl.ds(at, step)])
         for source, target, step in (
             (act_hbm, act_ref, 304), (cot_hbm, cot_ref, 32), (mem_hbm, mem_ref, 24),
@@ -286,6 +288,7 @@
         load.start()
     ring = Ring(cot_all, ring_sems)
 
+    seed_load.wait()
     high, low = split(seed_ref[...])
     both = jnp.concatenate([high.astype(F32), low.astype(F32)], axis=0)
     packed = both.T.astype(BF16)
@@ -318,13 +321,13 @@
 
     pl.semaphore_wait(barrier, count)
     def first_blocks():
+        ring.send(0)
         act_copies.extend(
             start_exchange(
                 "y", lambda o: (act_ref.at[window(o)], act_all.at[y]),
                 act_sems.at[0], act_sems.at[1],
             )
         )
-        ring.send(0)
 
     def to_sibling(block, index):
         (_, device), = peers("core")
@@ -545,11 +548,12 @@
             pltpu.VMEM((3 * RANK, DOUT), BF16),
             pltpu.VMEM((RANK, COLS), F32),
         ),
-        in_specs=[pl.BlockSpec(memory_space=pltpu.SMEM), vmem]
-        + [pl.BlockSpec(memory_space=pltpu.HBM)] * 3
-        + [vmem],
+        in_specs=[pl.BlockSpec(memory_space=pltpu.HBM)] * 6,
         out_specs=(vmem,) * 4,
         scratch_shapes=[
+            pltpu.SMEM((1,), jnp.int32),
+            pltpu.VMEM(gate_table.shape, F32),
+            pltpu.VMEM((RANK, COLS), F32),
             pltpu.VMEM((128, DOUT), BF16),
             pltpu.VMEM((DIN, 128), BF16),
             pltpu.VMEM((ROWS, DOUT), F32),
@@ -570,7 +574,7 @@
         + plan_scratch(LEFT_PLAN)
         + plan_scratch(RIGHT_PLAN)
         + [
-            pltpu.SemaphoreType.DMA((16,)),
+            pltpu.SemaphoreType.DMA((18,)),
             pltpu.SemaphoreType.DMA((2, 2, 8)),
             pltpu.SemaphoreType.DMA((2, 7)),
             pltpu.SemaphoreType.DMA((2, 2, 7)),

time: 92.4 us -> 91.9 us (level)
  no operation moved by 1% of the time
where the time goes in v6:
time: 91.9 us; the launch traced here: 91.7 us
  Pallas kernels  90.4 us (98%)
  between operations  1.28 us (1%)
    pallas_call x1, Pallas kernels, factors(): pl.pallas_call(kernel, out_shape=(pltpu.VMEM((ROWS, DOUT), F32), pltpu.VM...  89.1 us

profile of v6, /device:TPU:1, one launch (start us, length us, event | category | flops | bytes accessed | tf_op | source)
XLA Modules:
  0.0 91.7 jit_solution(16622432107671405098)
XLA Ops:
  1.3 89.1 %shard_map.77 = (f32[152,2432]{1,0:T(8,128)S(1)}, bf16[152,192]{1,0:T(8,128)(2,1)S(1)}, bf16[192,2432]{1,0:T(8,128)(2,1)S(1)}, f32[64,304]{1,0:T(8,128)S(1)}) custom-call(s32[1]{0:T(128)S(6)} %copy.8.step_hbm, f32[16,2432]{1,0:T(8,128)} %table_hbm.1, bf16[128,2432]{1,0:T(8,128)(2,1)} %bitcast.9, bf16[1216,128]{1,0:T(8,128)(2,1)} %bitcast.10, ...), custom_call_target="tpu_custom_call" | custom-call | tf_op jit(solution)/shard_map/pallas_call | solution.py:543
  90.4 1.4 %shard_map.78 = (f32[152,2432]{1,0:T(8,128)}, f32[64,304]{1,0:T(8,128)}) custom-call(f32[152,2432]{1,0:T(8,128)S(1)} %get-tuple-element.8.merged_ref, bf16[152,192]{1,0:T(8,128)(2,1)S(1)} %get-tuple-element.9.ortho_ref, bf16[192,2432]{1,0:T(8,128)(2,1)S(1)} %get-tuple-element.10.parts_ref, f32[64,304]{1,0:T(8,128)S(1)} %get-tuple-element.11.factor_ref), custom_call_target="tpu_custom_call" | custom-call | tf_op jit(solution)/shard_map/pallas_call | solution.py:608

commit v7 on v6

--- a/solution.py
+++ b/solution.py
@@ -68,8 +68,10 @@
             device_id=device,
             device_id_type=MESH,
         )
-        copy.start()
         copies.append(copy)
+    middle = (len(copies) - 1) / 2
+    for index in sorted(range(len(copies)), key=lambda at: abs(at - middle)):
+        copies[index].start()
     return copies
 
 
@@ -265,7 +267,7 @@
     x, z, c, y = place()
     barrier = pltpu.get_barrier_semaphore()
     count = 0
-    for axis in ("core", "x", "z", "y"):
+    for axis in ("z", "y", "x", "core"):
         for _, device in peers(axis):
             pl.semaphore_signal(barrier, inc=1, device_id=device, device_id_type=MESH)
             count += 1

time: 91.9 us -> 91.6 us (level)
  no operation moved by 1% of the time
where the time goes in v7:
time: 91.6 us; the launch traced here: 91.4 us
  Pallas kernels  90.2 us (98%)
  between operations  1.28 us (1%)
    pallas_call x1, Pallas kernels, factors(): pl.pallas_call(kernel, out_shape=(pltpu.VMEM((ROWS, DOUT), F32), pltpu.VM...  88.8 us

profile of v7, /device:TPU:1, one launch (start us, length us, event | category | flops | bytes accessed | tf_op | source)
XLA Modules:
  0.0 91.4 jit_solution(12261237674006230977)
XLA Ops:
  1.3 88.8 %shard_map.77 = (f32[152,2432]{1,0:T(8,128)S(1)}, bf16[152,192]{1,0:T(8,128)(2,1)S(1)}, bf16[192,2432]{1,0:T(8,128)(2,1)S(1)}, f32[64,304]{1,0:T(8,128)S(1)}) custom-call(s32[1]{0:T(128)S(6)} %copy.8.step_hbm, f32[16,2432]{1,0:T(8,128)} %table_hbm.1, bf16[128,2432]{1,0:T(8,128)(2,1)} %bitcast.9, bf16[1216,128]{1,0:T(8,128)(2,1)} %bitcast.10, ...), custom_call_target="tpu_custom_call" | custom-call | tf_op jit(solution)/shard_map/pallas_call | solution.py:545
  90.1 1.4 %shard_map.78 = (f32[152,2432]{1,0:T(8,128)}, f32[64,304]{1,0:T(8,128)}) custom-call(f32[152,2432]{1,0:T(8,128)S(1)} %get-tuple-element.8.merged_ref, bf16[152,192]{1,0:T(8,128)(2,1)S(1)} %get-tuple-element.9.ortho_ref, bf16[192,2432]{1,0:T(8,128)(2,1)S(1)} %get-tuple-element.10.parts_ref, f32[64,304]{1,0:T(8,128)S(1)} %get-tuple-element.11.factor_ref), custom_call_target="tpu_custom_call" | custom-call | tf_op jit(solution)/shard_map/pallas_call | solution.py:610
